TPU v7x, 32 devices: a whole 2x2x4 slice. The times are simulated.
32 devices in a mesh: wide: 16 (over z, y, core), narrow: 2 (over x).
Axes of the slice: x: 2, y: 2, z: 4, core: 2. Of those that a mesh axis runs over, the one named last changes fastest.
Arguments:
- right_side: float32 [96, 128, 256], P(('wide', 'narrow')), may hold values from -6 to 6
- diag_inverse: float32 [96, 128, 128], P(('wide', 'narrow')), may hold values from -1 to 1, as said below
- off_tiles: float32 [96, 48, 128, 128], P('wide', 'narrow'), may hold values from -0.078125 to 0.078125
- tile_columns: int32 [96, 48], P('wide', 'narrow'), may hold values from 0 to 95, as said below
- colors: int32 [96], replicated, may hold values from 0 to 2, as said below
Outputs:
- potentials: float32 [96, 128, 256], P(('wide', 'narrow'))
Inputs may be any that keep to these rules, and one draw needn't show every extreme that they name: `colors`: each device along wide+narrow owns 3 consecutive blocks, exactly 1 of each color. `tile_columns`: slot k of a block row names a block owned by a device whose narrow index is k // 24, and of another color than the row's block. `diag_inverse`: symmetric tiles.
All inputs are finite; a program needn't handle non-finite values.
Results may differ from a plain program's by a relative error of at most 0.0001.
Values sent between devices are 32-bit elements; how exact they have to be, the bound alone decides.
A program may use at most 128 MiB of HBM per device.

v0:
```python
from functools import partial
import jax
import jax.numpy as jnp
from jax import lax
from jax.sharding import PartitionSpec as P


def block_terms(stack, tile_rows, column_slots, column_hues, start, count):
    picked = stack[column_hues, column_slots]
    return jnp.einsum("rkab,rkbl->ral", tile_rows, picked, precision=lax.Precision.HIGHEST)


def sweep(source, sorted_inv, sorted_tiles, slot_of, color_of, wide_size, narrow_size, per_color):
    label_width = source.shape[2]
    tile_size = source.shape[1]
    copies = jnp.zeros((3, wide_size * per_color, tile_size, label_width), jnp.float32)
    pieces = [None, None, None]
    for section, color_now in enumerate((0, 1, 2, 1, 0)):
        offset = color_now * per_color
        local_side = source[offset : offset + per_color]
        if section > 0:
            row_low = color_now * narrow_size * per_color
            row_high = row_low + narrow_size * per_color
            term_fn = partial(
                block_terms,
                copies,
                sorted_tiles[row_low:row_high],
                slot_of[row_low:row_high],
                color_of[row_low:row_high],
            )
            summed = lax.psum_scatter(
                term_fn(jnp.int32(0), lax.axis_size("narrow") * per_color),
                "narrow",
                scatter_dimension=0,
                tiled=True,
            )
            local_side = local_side - summed
        updated = jnp.einsum(
            "rab,rbl->ral",
            sorted_inv[offset : offset + per_color],
            local_side,
            precision=lax.Precision.HIGHEST,
        )
        pieces[color_now] = updated
        if section < 4:
            gathered = lax.all_gather(updated, "wide", axis=0, tiled=True)
            copies = copies.at[color_now].set(gathered)
    return jnp.concatenate(pieces, axis=0)


def shards(right_side, diag_inverse, off_tiles, tile_columns, colors):
    wide_size = lax.axis_size("wide")
    narrow_size = lax.axis_size("narrow")
    wide_at = lax.axis_index("wide")
    narrow_at = lax.axis_index("narrow")
    row_count = off_tiles.shape[0]
    own_count = right_side.shape[0]
    per_color = own_count // 3
    block_total = colors.shape[0]
    row_colors = lax.dynamic_slice_in_dim(colors, wide_at * row_count, row_count)
    row_order = jnp.argsort(row_colors, stable=True)
    sorted_tiles = off_tiles[row_order]
    sorted_cols = tile_columns[row_order]
    owner_colors = colors.reshape(block_total // own_count, own_count)
    owner_order = jnp.argsort(owner_colors, axis=1, stable=True)
    owner_inverse = jnp.argsort(owner_order, axis=1)
    ranks = (owner_inverse - owner_colors * per_color).reshape(block_total)
    block_ids = jnp.arange(block_total, dtype=jnp.int32)
    slot_all = block_ids // (narrow_size * own_count) * per_color + ranks
    slot_of = slot_all[sorted_cols]
    color_of = colors[sorted_cols]
    own_start = (wide_at * narrow_size + narrow_at) * own_count
    own_colors = lax.dynamic_slice_in_dim(colors, own_start, own_count)
    own_order = jnp.argsort(own_colors, stable=True)
    own_inverse = jnp.argsort(own_order)
    sorted_inv = diag_inverse[own_order]
    sorted_side = right_side[own_order]
    result = sweep(
        sorted_side, sorted_inv, sorted_tiles, slot_of, color_of, wide_size, narrow_size, per_color
    )
    return result[own_inverse]


def solution(mesh):
    return jax.shard_map(
        shards,
        mesh=mesh,
        in_specs=(
            P(("wide", "narrow"), None, None),
            P(("wide", "narrow"), None, None),
            P("wide", "narrow", None, None),
            P("wide", "narrow"),
            P(),
        ),
        out_specs=P(("wide", "narrow"), None, None),
        check_vma=False,
    )
```

profile of v0, /device:TPU:0, one launch (start us, length us, event | category | flops | bytes accessed | tf_op | source)
XLA Modules:
  0.0 317.8 jit_solution(14142655278700782819)
XLA Ops:
  8.7 1.5 gather_fusion
  10.2 0.9 fusion.8
  12.7 1.0 sort.86
  13.7 1.2 gather_fusion.3
  16.6 1.9 gather_fusion.4
  18.6 1.6 gather_fusion.5
  20.5 8.6 %gather_fusion.2 = f32[6,24,128,128]{3,2,1,0:T(8,128)} fusion(f32[6,24,128,128]{3,2,1,0:T(8,128)} %param.15, s32[1024]{0:T(1024)S(1)} %pad_clamp_fusion.2), kind=kCustom, calls=%fused_computation.2 | custom fusion | bytes 18874392 | tf_op jit(solution)/shard_map/gather | solution.py:62
  29.1 26.3 %all-gather.9.cloned.1.call-done = f32[2048,256]{1,0:T(8,128)} async-done(((f32[128,256]{1,0:T(8,128)}), f32[2048,256]{1,0:T(8,128)}) %all-gather.9.cloned.1.call-update) | async-done | bytes 2097168 | tf_op jit(solution)/shard_map/all_gather | solution.py:46
  55.4 5.1 %scatter.14 = f32[3,16,128,256]{3,2,1,0:T(8,128)} pad(f32[1,16,128,256]{3,2,1,0:T(8,128)} %bitcast.69, f32[]{:T(128)} %constant.133.clone.1), padding=0_2x0_0x0_0x0_0 | pad | bytes 8388612 | tf_op jit(solution)/shard_map/scatter | solution.py:47
  60.4 6.5 %gather_fusion.6 = f32[48,128,256]{2,1,0:T(8,128)} fusion(f32[3,16,128,256]{3,2,1,0:T(8,128)} %scatter.14, s32[48]{0:T(128)S(1)} %reshape.253), kind=kCustom, calls=%fused_computation.6 | custom fusion | bytes 12583296 | tf_op jit(solution)/shard_map/gather | solution.py:9
  66.9 9.7 %convolution_bitcast_fusion.3 = f32[2,128,256]{2,1,0:T(8,128)} fusion(f32[6,24,128,128]{3,2,1,0:T(8,128)} %gather_fusion.2, f32[2,24,128,256]{3,2,1,0:T(8,128)} %bitcast.65), kind=kOutput, calls=%fused_computation.14 | convolution fusion | flops 2415919104 | bytes 15990784 | tf_op jit(solution)/shard_map/rkab,rkbl->ral/dot_general | solution.py:10
  76.7 10.5 %reduce-scatter.5.cloned.1.call-done = f32[1,128,256]{2,1,0:T(8,128)} async-done(((f32[2,128,256]{2,1,0:T(8,128)}), f32[1,128,256]{2,1,0:T(8,128)}) %reduce-scatter.5.cloned.1.call-update) | async-done | bytes 131088 | tf_op jit(solution)/shard_map/reduce_scatter | solution.py:31
  87.3 1.8 fusion.6
  89.4 41.7 %all-gather.11.cloned.1.call-done = f32[2048,256]{1,0:T(8,128)} async-done(((f32[128,256]{1,0:T(8,128)}), f32[2048,256]{1,0:T(8,128)}) %all-gather.11.cloned.1.call-update) | async-done | bytes 2097168 | tf_op jit(solution)/shard_map/all_gather | solution.py:46
  131.1 3.2 %constant_dynamic-update-slice_fusion.2 = f32[3,16,128,256]{3,2,1,0:T(8,128)} fusion(f32[3,16,128,256]{3,2,1,0:T(8,128)} %scatter.14, f32[1,16,128,256]{3,2,1,0:T(8,128)} %bitcast.67), kind=kLoop, calls=%fused_computation.72 | loop fusion | bytes 4194304 | tf_op jit(solution)/shard_map/scatter | solution.py:47
  134.3 6.5 %gather_fusion.7 = f32[48,128,256]{2,1,0:T(8,128)} fusion(f32[3,16,128,256]{3,2,1,0:T(8,128)} %constant_dynamic-update-slice_fusion.2, s32[48]{0:T(128)S(1)} %reshape.259), kind=kCustom, calls=%fused_computation.7 | custom fusion | bytes 12583296 | tf_op jit(solution)/shard_map/gather | solution.py:9
  140.8 9.7 %convolution_bitcast_fusion.2 = f32[2,128,256]{2,1,0:T(8,128)} fusion(f32[6,24,128,128]{3,2,1,0:T(8,128)} %gather_fusion.2, f32[2,24,128,256]{3,2,1,0:T(8,128)} %bitcast.63), kind=kOutput, calls=%fused_computation.13 | convolution fusion | flops 2415919104 | bytes 15990784 | tf_op jit(solution)/shard_map/rkab,rkbl->ral/dot_general | solution.py:10
  150.6 10.5 %reduce-scatter.7.cloned.1.call-done = f32[1,128,256]{2,1,0:T(8,128)} async-done(((f32[2,128,256]{2,1,0:T(8,128)}), f32[1,128,256]{2,1,0:T(8,128)}) %reduce-scatter.7.cloned.1.call-update) | async-done | bytes 131088 | tf_op jit(solution)/shard_map/reduce_scatter | solution.py:31
  161.2 1.8 fusion.1
  163.2 41.4 %all-gather.13.cloned.1.call-done = f32[2048,256]{1,0:T(8,128)} async-done(((f32[128,256]{1,0:T(8,128)}), f32[2048,256]{1,0:T(8,128)}) %all-gather.13.cloned.1.call-update) | async-done | bytes 2097168 | tf_op jit(solution)/shard_map/all_gather | solution.py:46
  204.6 3.1 constant_dynamic-update-slice_fusion.1
  207.7 6.5 %gather_fusion.8 = f32[48,128,256]{2,1,0:T(8,128)} fusion(f32[3,16,128,256]{3,2,1,0:T(8,128)} %constant_dynamic-update-slice_fusion.1, s32[48]{0:T(128)S(1)} %reshape.253), kind=kCustom, calls=%fused_computation.8 | custom fusion | bytes 12583296 | tf_op jit(solution)/shard_map/gather | solution.py:9
  214.2 9.7 %convolution_bitcast_fusion.1 = f32[2,128,256]{2,1,0:T(8,128)} fusion(f32[6,24,128,128]{3,2,1,0:T(8,128)} %gather_fusion.2, f32[2,24,128,256]{3,2,1,0:T(8,128)} %bitcast.64), kind=kOutput, calls=%fused_computation.12 | convolution fusion | flops 2415919104 | bytes 15990784 | tf_op jit(solution)/shard_map/rkab,rkbl->ral/dot_general | solution.py:10
  224.0 10.5 %reduce-scatter.9.cloned.1.call-done = f32[1,128,256]{2,1,0:T(8,128)} async-done(((f32[2,128,256]{2,1,0:T(8,128)}), f32[1,128,256]{2,1,0:T(8,128)}) %reduce-scatter.9.cloned.1.call-update) | async-done | bytes 131088 | tf_op jit(solution)/shard_map/reduce_scatter | solution.py:31
  234.5 1.8 fusion.4
  236.7 41.7 %all-gather.15.cloned.1.call-done = f32[2048,256]{1,0:T(8,128)} async-done(((f32[128,256]{1,0:T(8,128)}), f32[2048,256]{1,0:T(8,128)}) %all-gather.15.cloned.1.call-update) | async-done | bytes 2097168 | tf_op jit(solution)/shard_map/all_gather | solution.py:46
  278.4 3.2 %constant_dynamic-update-slice_fusion = f32[3,16,128,256]{3,2,1,0:T(8,128)} fusion(f32[3,16,128,256]{3,2,1,0:T(8,128)} %constant_dynamic-update-slice_fusion.1, f32[1,16,128,256]{3,2,1,0:T(8,128)} %bitcast.66), kind=kLoop, calls=%fused_computation.70 | loop fusion | bytes 4194304 | tf_op jit(solution)/shard_map/scatter | solution.py:47
  281.6 6.5 %gather_fusion.9 = f32[48,128,256]{2,1,0:T(8,128)} fusion(f32[3,16,128,256]{3,2,1,0:T(8,128)} %constant_dynamic-update-slice_fusion, s32[48]{0:T(128)S(1)} %reshape.271), kind=kCustom, calls=%fused_computation.9 | custom fusion | bytes 12583296 | tf_op jit(solution)/shard_map/gather | solution.py:9
  288.1 9.8 %convolution_bitcast_fusion = f32[2,128,256]{2,1,0:T(8,128)} fusion(f32[6,24,128,128]{3,2,1,0:T(8,128)} %gather_fusion.2, f32[2,24,128,256]{3,2,1,0:T(8,128)} %bitcast.62), kind=kOutput, calls=%fused_computation.11 | convolution fusion | flops 2415919104 | bytes 15990784 | tf_op jit(solution)/shard_map/rkab,rkbl->ral/dot_general | solution.py:10
  298.6 9.8 %reduce-scatter.11.cloned.1.call-done = f32[1,128,256]{2,1,0:T(8,128)} async-done(((f32[2,128,256]{2,1,0:T(8,128)}), f32[1,128,256]{2,1,0:T(8,128)}) %reduce-scatter.11.cloned.1.call-update) | async-done | bytes 131088 | tf_op jit(solution)/shard_map/reduce_scatter | solution.py:31
  308.5 1.2 convolution_bitcast_fusion.4
  309.7 1.3 gather_fusion.10
  (64 shorter events, 7.6 us)
Async XLA Ops:
  6.5 1.6 copy-start
  6.5 48.8 %all-gather.9.cloned.1.call-start = ((), (), s32[]{:S(2)}) async-start(), calls=%async_computation.8 | async-start | bytes 2228224 | tf_op jit(solution)/shard_map/all_gather | solution.py:46
  11.1 76.2 %reduce-scatter.5.cloned.1.call-start = ((), (), s32[]{:S(2)}) async-start(), calls=%async_computation.4 | async-start | bytes 393216 | tf_op jit(solution)/shard_map/reduce_scatter | solution.py:31
  76.7 54.4 %all-gather.11.cloned.1.call-start = ((), (), s32[]{:S(2)}) async-start(), calls=%async_computation.9 | async-start | bytes 2228224 | tf_op jit(solution)/shard_map/all_gather | solution.py:46
  89.1 72.1 %reduce-scatter.7.cloned.1.call-start = ((), (), s32[]{:S(2)}) async-start(), calls=%async_computation.5 | async-start | bytes 393216 | tf_op jit(solution)/shard_map/reduce_scatter | solution.py:31
  150.6 54.0 %all-gather.13.cloned.1.call-start = ((), (), s32[]{:S(2)}) async-start(), calls=%async_computation.10 | async-start | bytes 2228224 | tf_op jit(solution)/shard_map/all_gather | solution.py:46
  163.0 71.5 %reduce-scatter.9.cloned.1.call-start = ((), (), s32[]{:S(2)}) async-start(), calls=%async_computation.6 | async-start | bytes 393216 | tf_op jit(solution)/shard_map/reduce_scatter | solution.py:31
  223.9 54.4 %all-gather.15.cloned.1.call-start = ((), (), s32[]{:S(2)}) async-start(), calls=%async_computation.11 | async-start | bytes 2228224 | tf_op jit(solution)/shard_map/all_gather | solution.py:46
  236.4 72.1 %reduce-scatter.11.cloned.1.call-start = ((), (), s32[]{:S(2)}) async-start(), calls=%async_computation.7 | async-start | bytes 393216 | tf_op jit(solution)/shard_map/reduce_scatter | solution.py:31
  288.1 21.6 %copy-start.1 = (f32[128,256]{1,0:T(8,128)S(1)}, f32[128,256]{1,0:T(8,128)}, u32[]{:S(2)}) copy-start(f32[128,256]{1,0:T(8,128)} %fusion.1) | copy-start | bytes 393220
  288.1 21.6 %copy-start.2 = (f32[128,256]{1,0:T(8,128)S(1)}, f32[128,256]{1,0:T(8,128)}, u32[]{:S(2)}) copy-start(f32[128,256]{1,0:T(8,128)} %fusion.4) | copy-start | bytes 393220
Sparse Core Ops, SparseCore 0:
  11.2 44.0 all-gather.8
  76.8 10.4 reduce-scatter.4
  89.7 41.4 all-gather.10
  150.7 10.4 reduce-scatter.6
  163.2 41.3 all-gather.12
  224.1 10.4 reduce-scatter.8
  236.9 41.4 all-gather.14
  298.0 10.4 reduce-scatter.10
where the time goes:
time: 318 us
  waiting for transfers between devices  193 us (61%)
  local copies, waits for them, and re-layouts  60.7 us (19%)
  matrix products  46.6 us (15%)
  between operations  13.6 us (4%)
  other arithmetic  3.94 us (1%)
    all_gather x4, waiting for transfers between devices, sweep(): gathered = lax.all_gather(updated, 'wide', axis=0, tiled=True)  151 us
    reduce_scatter x4, waiting for transfers between devices, sweep(): lax.psum_scatter(term_fn(jnp.int32(0), lax.axis_size('narrow') * per_colo...  41.4 us
    dot_general x4, matrix products, block_terms(): jnp.einsum('rkab,rkbl->ral', tile_rows, picked, precision=lax.Precision.H...  39 us
    gather x4, local copies, waits for them, and re-layouts, block_terms(): picked = stack[column_hues, column_slots]  26 us
    scatter x4, local copies, waits for them, and re-layouts, sweep(): copies = copies.at[color_now].set(gathered)  14.5 us
    gather x1, local copies, waits for them, and re-layouts, shards(): sorted_tiles = off_tiles[row_order]  8.58 us
    dot_general x5, matrix products, sweep(): jnp.einsum('rab,rbl->ral', sorted_inv[offset:offset + per_color], local_s...  7.55 us
  transfers between devices with their start and end apart: 8, of which 8 were waited for; matrix products, arithmetic and copies ran while one was open for 6% of the time, Pallas kernels for 0%

commit v1 on v0

--- a/solution.py
+++ b/solution.py
@@ -43,7 +43,26 @@
         )
         pieces[color_now] = updated
         if section < 4:
-            gathered = lax.all_gather(updated, "wide", axis=0, tiled=True)
+            ways, here, step = (lax.axis_size("wide"), lax.axis_index("wide"), updated.shape[0])
+            dims = [n * ways if d == 0 else n for d, n in enumerate(updated.shape)]
+            gathered = lax.dynamic_update_slice_in_dim(
+                jnp.zeros(dims, updated.dtype), updated, here * step, axis=0
+            )
+            going_up = going_down = updated
+            for far in range(1, ways // 2 + 1):
+                going_up = lax.ppermute(
+                    going_up, "wide", [(d, (d + 1) % ways) for d in range(ways)]
+                )
+                gathered = lax.dynamic_update_slice_in_dim(
+                    gathered, going_up, (here - far) % ways * step, axis=0
+                )
+                if 2 * far < ways:
+                    going_down = lax.ppermute(
+                        going_down, "wide", [(d, (d - 1) % ways) for d in range(ways)]
+                    )
+                    gathered = lax.dynamic_update_slice_in_dim(
+                        gathered, going_down, (here + far) % ways * step, axis=0
+                    )
             copies = copies.at[color_now].set(gathered)
     return jnp.concatenate(pieces, axis=0)
 

time: 318 us -> 373 us (1.17)
  starting transfers between devices: 0.48 us -> 127 us
  waiting for transfers between devices: 193 us -> 131 us
  matrix products: 46.6 us -> 41.2 us
  local copies, waits for them, and re-layouts: 60.7 us -> 55.5 us
    all_gather x4 -> x0, waiting for transfers between devices: 151 us -> none  [sweep(): gathered = lax.all_gather(updated, 'wide', axis=0, tiled=True)]
    ppermute x0 -> x60, starting transfers between devices: none -> 127 us  [the longest x28 126 us: sweep(): lax.ppermute(going_down, 'wide', [(d, (d - 1) % ways) for d in range(ways)])]
    ppermute x0 -> x60, waiting for transfers between devices: none -> 98.9 us  [the longest x32 98.7 us: sweep(): lax.ppermute(going_up, 'wide', [(d, (d + 1) % ways) for d in range(ways)])]
    reduce_scatter x4, waiting for transfers between devices: 41.4 us -> 31.9 us  [sweep(): lax.psum_scatter(term_fn(jnp.int32(0), lax.axis_size('narrow') * per_colo...]
    scatter x4, local copies, waits for them, and re-layouts: 14.5 us -> 8.05 us  [sweep(): copies = copies.at[color_now].set(gathered)]
    dot_general x5, matrix products: 7.55 us -> 2.2 us  [sweep(): jnp.einsum('rab,rbl->ral', sorted_inv[offset:offset + per_color], local_s...]
  transfers between devices with their start and end apart: 8 -> 64, of which waited for: 8 -> 36; matrix products, arithmetic and copies ran while one was open for 6% -> 5% of each run, Pallas kernels for 0% -> 0%
where the time goes in v1:
time: 373 us
  waiting for transfers between devices  131 us (35%)
  starting transfers between devices  127 us (34%)
  local copies, waits for them, and re-layouts  55.5 us (15%)
  matrix products  41.2 us (11%)
  between operations  13.8 us (4%)
  other arithmetic  3.86 us (1%)
    ppermute x28, starting transfers between devices, sweep(): lax.ppermute(going_down, 'wide', [(d, (d - 1) % ways) for d in range(ways)])  126 us
    ppermute x32, waiting for transfers between devices, sweep(): lax.ppermute(going_up, 'wide', [(d, (d + 1) % ways) for d in range(ways)])  98.7 us
    dot_general x4, matrix products, block_terms(): jnp.einsum('rkab,rkbl->ral', tile_rows, picked, precision=lax.Precision.H...  39 us
    reduce_scatter x4, waiting for transfers between devices, sweep(): lax.psum_scatter(term_fn(jnp.int32(0), lax.axis_size('narrow') * per_colo...  31.9 us
    gather x4, local copies, waits for them, and re-layouts, block_terms(): picked = stack[column_hues, column_slots]  26.1 us
    gather x1, local copies, waits for them, and re-layouts, shards(): sorted_tiles = off_tiles[row_order]  8.49 us
    scatter x4, local copies, waits for them, and re-layouts, sweep(): copies = copies.at[color_now].set(gathered)  8.05 us
  transfers between devices with their start and end apart: 64, of which 36 were waited for; matrix products, arithmetic and copies ran while one was open for 5% of the time, Pallas kernels for 0%

profile of v1, /device:TPU:0, one launch (start us, length us, event | category | flops | bytes accessed | tf_op | source)
XLA Modules:
  0.0 372.7 jit_solution(2985089520291559216)
XLA Ops:
  11.2 5.1 %collective-permute-start.1 = (f32[1,128,256]{2,1,0:T(8,128)S(1)}, f32[1,128,256]{2,1,0:T(8,128)S(1)}, u32[]{:S(2)}, u32[]{:S(2)}) collective-permute-start(f32[1,128,256]{2,1,0:T(8,128)S(1)} %bitcast.215), channel_id=1, source_target_pairs={{0,30},{2,0},{4,2},{6,4},{8,6},{10,8},{12,10},{14,12},{16,14},{18,... | collective-permute-start | bytes 393224 | tf_op jit(solution)/shard_map/ppermute | solution.py:60
  23.2 8.5 %gather_fusion.2 = f32[6,24,128,128]{3,2,1,0:T(8,128)} fusion(f32[6,24,128,128]{3,2,1,0:T(8,128)} %param.15, s32[1024]{0:T(1024)S(1)} %pad_clamp_fusion.2), kind=kCustom, calls=%fused_computation.2 | custom fusion | bytes 18874392 | tf_op jit(solution)/shard_map/gather | solution.py:81
  38.8 4.5 %collective-permute-start.5 = (f32[1,128,256]{2,1,0:T(8,128)S(1)}, f32[1,128,256]{2,1,0:T(8,128)S(1)}, u32[]{:S(2)}, u32[]{:S(2)}) collective-permute-start(f32[1,128,256]{2,1,0:T(8,128)S(1)} %collective-permute-done.3), channel_id=1, source_target_pairs={{0,30},{2,0},{4,2},{6,4},{8,6},{10,8},{12,10},{14,12},{16,14},{18,... | collective-permute-start | bytes 393224 | tf_op jit(solution)/shard_map/ppermute | solution.py:60
  74.7 7.0 %collective-permute-done.14 = f32[1,128,256]{2,1,0:T(8,128)S(1)} collective-permute-done((f32[1,128,256]{2,1,0:T(8,128)S(1)}, f32[1,128,256]{2,1,0:T(8,128)S(1)}, u32[]{:S(2)}, u32[]{:S(2)}) %collective-permute-start.14) | collective-permute-done | bytes 131104 | tf_op jit(solution)/shard_map/ppermute | solution.py:53
  85.1 6.5 %gather_fusion.6 = f32[48,128,256]{2,1,0:T(8,128)} fusion(f32[3,16,128,256]{3,2,1,0:T(8,128)} %scatter.14, s32[48]{0:T(128)S(1)} %reshape.936), kind=kCustom, calls=%fused_computation.6 | custom fusion | bytes 12583296 | tf_op jit(solution)/shard_map/gather | solution.py:9
  91.6 9.7 %convolution_bitcast_fusion.3 = f32[2,128,256]{2,1,0:T(8,128)} fusion(f32[6,24,128,128]{3,2,1,0:T(8,128)} %gather_fusion.2, f32[2,24,128,256]{3,2,1,0:T(8,128)} %bitcast.207), kind=kOutput, calls=%fused_computation.14 | convolution fusion | flops 2415919104 | bytes 15990784 | tf_op jit(solution)/shard_map/rkab,rkbl->ral/dot_general | solution.py:10
  101.6 9.3 %reduce-scatter.5.cloned.1.call-done = f32[1,128,256]{2,1,0:T(8,128)} async-done(((f32[2,128,256]{2,1,0:T(8,128)}), f32[1,128,256]{2,1,0:T(8,128)}) %reduce-scatter.5.cloned.1.call-update) | async-done | bytes 131088 | tf_op jit(solution)/shard_map/reduce_scatter | solution.py:31
  126.4 4.5 %collective-permute-start.20 = (f32[1,128,256]{2,1,0:T(8,128)S(1)}, f32[1,128,256]{2,1,0:T(8,128)S(1)}, u32[]{:S(2)}, u32[]{:S(2)}) collective-permute-start(f32[1,128,256]{2,1,0:T(8,128)S(1)} %collective-permute-done.18), channel_id=1, source_target_pairs={{0,30},{2,0},{4,2},{6,4},{8,6},{10,8},{12,10},{14,12},{16,14},{18,... | collective-permute-start | bytes 393224 | tf_op jit(solution)/shard_map/ppermute | solution.py:60
  133.6 4.5 %collective-permute-start.22 = (f32[1,128,256]{2,1,0:T(8,128)S(1)}, f32[1,128,256]{2,1,0:T(8,128)S(1)}, u32[]{:S(2)}, u32[]{:S(2)}) collective-permute-start(f32[1,128,256]{2,1,0:T(8,128)S(1)} %collective-permute-done.20), channel_id=1, source_target_pairs={{0,30},{2,0},{4,2},{6,4},{8,6},{10,8},{12,10},{14,12},{16,14},{18,... | collective-permute-start | bytes 393224 | tf_op jit(solution)/shard_map/ppermute | solution.py:60
  140.8 4.5 %collective-permute-start.24 = (f32[1,128,256]{2,1,0:T(8,128)S(1)}, f32[1,128,256]{2,1,0:T(8,128)S(1)}, u32[]{:S(2)}, u32[]{:S(2)}) collective-permute-start(f32[1,128,256]{2,1,0:T(8,128)S(1)} %collective-permute-done.22), channel_id=1, source_target_pairs={{0,30},{2,0},{4,2},{6,4},{8,6},{10,8},{12,10},{14,12},{16,14},{18,... | collective-permute-start | bytes 393224 | tf_op jit(solution)/shard_map/ppermute | solution.py:60
  148.0 4.5 %collective-permute-start.26 = (f32[1,128,256]{2,1,0:T(8,128)S(1)}, f32[1,128,256]{2,1,0:T(8,128)S(1)}, u32[]{:S(2)}, u32[]{:S(2)}) collective-permute-start(f32[1,128,256]{2,1,0:T(8,128)S(1)} %collective-permute-done.24), channel_id=1, source_target_pairs={{0,30},{2,0},{4,2},{6,4},{8,6},{10,8},{12,10},{14,12},{16,14},{18,... | collective-permute-start | bytes 393224 | tf_op jit(solution)/shard_map/ppermute | solution.py:60
  155.2 4.5 %collective-permute-start.28 = (f32[1,128,256]{2,1,0:T(8,128)S(1)}, f32[1,128,256]{2,1,0:T(8,128)S(1)}, u32[]{:S(2)}, u32[]{:S(2)}) collective-permute-start(f32[1,128,256]{2,1,0:T(8,128)S(1)} %collective-permute-done.26), channel_id=1, source_target_pairs={{0,30},{2,0},{4,2},{6,4},{8,6},{10,8},{12,10},{14,12},{16,14},{18,... | collective-permute-start | bytes 393224 | tf_op jit(solution)/shard_map/ppermute | solution.py:60
  162.3 7.0 %collective-permute-done.29 = f32[1,128,256]{2,1,0:T(8,128)S(1)} collective-permute-done((f32[1,128,256]{2,1,0:T(8,128)S(1)}, f32[1,128,256]{2,1,0:T(8,128)S(1)}, u32[]{:S(2)}, u32[]{:S(2)}) %collective-permute-start.29) | collective-permute-done | bytes 131104 | tf_op jit(solution)/shard_map/ppermute | solution.py:53
  171.0 6.5 %gather_fusion.7 = f32[48,128,256]{2,1,0:T(8,128)} fusion(f32[3,16,128,256]{3,2,1,0:T(8,128)} %constant_dynamic-update-slice_fusion.2, s32[48]{0:T(128)S(1)} %reshape.942), kind=kCustom, calls=%fused_computation.7 | custom fusion | bytes 12583296 | tf_op jit(solution)/shard_map/gather | solution.py:9
  177.5 9.7 %convolution_bitcast_fusion.2 = f32[2,128,256]{2,1,0:T(8,128)} fusion(f32[6,24,128,128]{3,2,1,0:T(8,128)} %gather_fusion.2, f32[2,24,128,256]{3,2,1,0:T(8,128)} %bitcast.205), kind=kOutput, calls=%fused_computation.13 | convolution fusion | flops 2415919104 | bytes 15990784 | tf_op jit(solution)/shard_map/rkab,rkbl->ral/dot_general | solution.py:10
  187.3 7.8 %reduce-scatter.7.cloned.1.call-done = f32[1,128,256]{2,1,0:T(8,128)} async-done(((f32[2,128,256]{2,1,0:T(8,128)}), f32[1,128,256]{2,1,0:T(8,128)}) %reduce-scatter.7.cloned.1.call-update) | async-done | bytes 131088 | tf_op jit(solution)/shard_map/reduce_scatter | solution.py:31
  225.1 4.5 %collective-permute-start.39 = (f32[1,128,256]{2,1,0:T(8,128)S(1)}, f32[1,128,256]{2,1,0:T(8,128)S(1)}, u32[]{:S(2)}, u32[]{:S(2)}) collective-permute-start(f32[1,128,256]{2,1,0:T(8,128)S(1)} %collective-permute-done.37), channel_id=1, source_target_pairs={{0,30},{2,0},{4,2},{6,4},{8,6},{10,8},{12,10},{14,12},{16,14},{18,... | collective-permute-start | bytes 393224 | tf_op jit(solution)/shard_map/ppermute | solution.py:60
  232.3 4.5 %collective-permute-start.41 = (f32[1,128,256]{2,1,0:T(8,128)S(1)}, f32[1,128,256]{2,1,0:T(8,128)S(1)}, u32[]{:S(2)}, u32[]{:S(2)}) collective-permute-start(f32[1,128,256]{2,1,0:T(8,128)S(1)} %collective-permute-done.39), channel_id=1, source_target_pairs={{0,30},{2,0},{4,2},{6,4},{8,6},{10,8},{12,10},{14,12},{16,14},{18,... | collective-permute-start | bytes 393224 | tf_op jit(solution)/shard_map/ppermute | solution.py:60
  239.5 4.5 %collective-permute-start.43 = (f32[1,128,256]{2,1,0:T(8,128)S(1)}, f32[1,128,256]{2,1,0:T(8,128)S(1)}, u32[]{:S(2)}, u32[]{:S(2)}) collective-permute-start(f32[1,128,256]{2,1,0:T(8,128)S(1)} %collective-permute-done.41), channel_id=1, source_target_pairs={{0,30},{2,0},{4,2},{6,4},{8,6},{10,8},{12,10},{14,12},{16,14},{18,... | collective-permute-start | bytes 393224 | tf_op jit(solution)/shard_map/ppermute | solution.py:60
  246.6 7.0 %collective-permute-done.44 = f32[1,128,256]{2,1,0:T(8,128)S(1)} collective-permute-done((f32[1,128,256]{2,1,0:T(8,128)S(1)}, f32[1,128,256]{2,1,0:T(8,128)S(1)}, u32[]{:S(2)}, u32[]{:S(2)}) %collective-permute-start.44) | collective-permute-done | bytes 131104 | tf_op jit(solution)/shard_map/ppermute | solution.py:53
  255.1 6.5 %gather_fusion.8 = f32[48,128,256]{2,1,0:T(8,128)} fusion(f32[3,16,128,256]{3,2,1,0:T(8,128)} %constant_dynamic-update-slice_fusion.1, s32[48]{0:T(128)S(1)} %reshape.936), kind=kCustom, calls=%fused_computation.8 | custom fusion | bytes 12583296 | tf_op jit(solution)/shard_map/gather | solution.py:9
  261.6 9.7 %convolution_bitcast_fusion.1 = f32[2,128,256]{2,1,0:T(8,128)} fusion(f32[6,24,128,128]{3,2,1,0:T(8,128)} %gather_fusion.2, f32[2,24,128,256]{3,2,1,0:T(8,128)} %bitcast.206), kind=kOutput, calls=%fused_computation.12 | convolution fusion | flops 2415919104 | bytes 15990784 | tf_op jit(solution)/shard_map/rkab,rkbl->ral/dot_general | solution.py:10
  271.6 7.7 %reduce-scatter.9.cloned.1.call-done = f32[1,128,256]{2,1,0:T(8,128)} async-done(((f32[2,128,256]{2,1,0:T(8,128)}), f32[1,128,256]{2,1,0:T(8,128)}) %reduce-scatter.9.cloned.1.call-update) | async-done | bytes 131088 | tf_op jit(solution)/shard_map/reduce_scatter | solution.py:31
  294.9 4.5 %collective-permute-start.50 = (f32[1,128,256]{2,1,0:T(8,128)S(1)}, f32[1,128,256]{2,1,0:T(8,128)S(1)}, u32[]{:S(2)}, u32[]{:S(2)}) collective-permute-start(f32[1,128,256]{2,1,0:T(8,128)S(1)} %collective-permute-done.48), channel_id=1, source_target_pairs={{0,30},{2,0},{4,2},{6,4},{8,6},{10,8},{12,10},{14,12},{16,14},{18,... | collective-permute-start | bytes 393224 | tf_op jit(solution)/shard_map/ppermute | solution.py:60
  302.1 4.5 %collective-permute-start.52 = (f32[1,128,256]{2,1,0:T(8,128)S(1)}, f32[1,128,256]{2,1,0:T(8,128)S(1)}, u32[]{:S(2)}, u32[]{:S(2)}) collective-permute-start(f32[1,128,256]{2,1,0:T(8,128)S(1)} %collective-permute-done.50), channel_id=1, source_target_pairs={{0,30},{2,0},{4,2},{6,4},{8,6},{10,8},{12,10},{14,12},{16,14},{18,... | collective-permute-start | bytes 393224 | tf_op jit(solution)/shard_map/ppermute | solution.py:60
  309.2 4.5 %collective-permute-start.54 = (f32[1,128,256]{2,1,0:T(8,128)S(1)}, f32[1,128,256]{2,1,0:T(8,128)S(1)}, u32[]{:S(2)}, u32[]{:S(2)}) collective-permute-start(f32[1,128,256]{2,1,0:T(8,128)S(1)} %collective-permute-done.52), channel_id=1, source_target_pairs={{0,30},{2,0},{4,2},{6,4},{8,6},{10,8},{12,10},{14,12},{16,14},{18,... | collective-permute-start | bytes 393224 | tf_op jit(solution)/shard_map/ppermute | solution.py:60
  316.4 4.7 %collective-permute-start.56 = (f32[1,128,256]{2,1,0:T(8,128)S(1)}, f32[1,128,256]{2,1,0:T(8,128)S(1)}, u32[]{:S(2)}, u32[]{:S(2)}) collective-permute-start(f32[1,128,256]{2,1,0:T(8,128)S(1)} %collective-permute-done.54), channel_id=1, source_target_pairs={{0,30},{2,0},{4,2},{6,4},{8,6},{10,8},{12,10},{14,12},{16,14},{18,... | collective-permute-start | bytes 393224 | tf_op jit(solution)/shard_map/ppermute | solution.py:60
  323.7 4.7 %collective-permute-start.58 = (f32[1,128,256]{2,1,0:T(8,128)S(1)}, f32[1,128,256]{2,1,0:T(8,128)S(1)}, u32[]{:S(2)}, u32[]{:S(2)}) collective-permute-start(f32[1,128,256]{2,1,0:T(8,128)S(1)} %collective-permute-done.56), channel_id=1, source_target_pairs={{0,30},{2,0},{4,2},{6,4},{8,6},{10,8},{12,10},{14,12},{16,14},{18,... | collective-permute-start | bytes 393224 | tf_op jit(solution)/shard_map/ppermute | solution.py:60
  330.9 6.9 %collective-permute-done.59 = f32[1,128,256]{2,1,0:T(8,128)S(1)} collective-permute-done((f32[1,128,256]{2,1,0:T(8,128)S(1)}, f32[1,128,256]{2,1,0:T(8,128)S(1)}, u32[]{:S(2)}, u32[]{:S(2)}) %collective-permute-start.59) | collective-permute-done | bytes 131104 | tf_op jit(solution)/shard_map/ppermute | solution.py:53
  339.4 6.5 %gather_fusion.9 = f32[48,128,256]{2,1,0:T(8,128)} fusion(f32[3,16,128,256]{3,2,1,0:T(8,128)} %constant_dynamic-update-slice_fusion, s32[48]{0:T(128)S(1)} %reshape.954), kind=kCustom, calls=%fused_computation.9 | custom fusion | bytes 12583296 | tf_op jit(solution)/shard_map/gather | solution.py:9
  345.9 9.8 %convolution_bitcast_fusion = f32[2,128,256]{2,1,0:T(8,128)} fusion(f32[6,24,128,128]{3,2,1,0:T(8,128)} %gather_fusion.2, f32[2,24,128,256]{3,2,1,0:T(8,128)} %bitcast.204), kind=kOutput, calls=%fused_computation.11 | convolution fusion | flops 2415919104 | bytes 15990784 | tf_op jit(solution)/shard_map/rkab,rkbl->ral/dot_general | solution.py:10
  356.5 7.1 %reduce-scatter.11.cloned.1.call-done = f32[1,128,256]{2,1,0:T(8,128)} async-done(((f32[2,128,256]{2,1,0:T(8,128)}), f32[1,128,256]{2,1,0:T(8,128)}) %reduce-scatter.11.cloned.1.call-update) | async-done | bytes 131088 | tf_op jit(solution)/shard_map/reduce_scatter | solution.py:31
  (244 shorter events, 156.8 us)
Async XLA Ops:
  6.5 104.3 %reduce-scatter.5.cloned.1.call-start = ((), (), s32[]{:S(2)}) async-start(), calls=%async_computation.4 | async-start | bytes 393216 | tf_op jit(solution)/shard_map/reduce_scatter | solution.py:31
  10.7 21.0 %collective-permute-start = (f32[1,128,256]{2,1,0:T(8,128)S(1)}, f32[1,128,256]{2,1,0:T(8,128)S(1)}, u32[]{:S(2)}, u32[]{:S(2)}) collective-permute-start(f32[1,128,256]{2,1,0:T(8,128)S(1)} %bitcast.214), channel_id=1, source_target_pairs={{0,2},{2,4},{4,6},{6,8},{8,10},{10,12},{12,14},{14,16},{16,18},{18... | collective-permute-start | bytes 393224 | tf_op jit(solution)/shard_map/ppermute | solution.py:53
  11.2 20.5 %collective-permute-start.1 = (f32[1,128,256]{2,1,0:T(8,128)S(1)}, f32[1,128,256]{2,1,0:T(8,128)S(1)}, u32[]{:S(2)}, u32[]{:S(2)}) collective-permute-start(f32[1,128,256]{2,1,0:T(8,128)S(1)} %bitcast.215), channel_id=1, source_target_pairs={{0,30},{2,0},{4,2},{6,4},{8,6},{10,8},{12,10},{14,12},{16,14},{18,... | collective-permute-start | bytes 393224 | tf_op jit(solution)/shard_map/ppermute | solution.py:60
  38.8 7.2 %collective-permute-start.4 = (f32[1,128,256]{2,1,0:T(8,128)S(1)}, f32[1,128,256]{2,1,0:T(8,128)S(1)}, u32[]{:S(2)}, u32[]{:S(2)}) collective-permute-start(f32[1,128,256]{2,1,0:T(8,128)S(1)} %collective-permute-done.2), channel_id=1, source_target_pairs={{0,2},{2,4},{4,6},{6,8},{8,10},{10,12},{12,14},{14,16},{16,18},{18... | collective-permute-start | bytes 393224 | tf_op jit(solution)/shard_map/ppermute | solution.py:53
  38.8 7.2 %collective-permute-start.5 = (f32[1,128,256]{2,1,0:T(8,128)S(1)}, f32[1,128,256]{2,1,0:T(8,128)S(1)}, u32[]{:S(2)}, u32[]{:S(2)}) collective-permute-start(f32[1,128,256]{2,1,0:T(8,128)S(1)} %collective-permute-done.3), channel_id=1, source_target_pairs={{0,30},{2,0},{4,2},{6,4},{8,6},{10,8},{12,10},{14,12},{16,14},{18,... | collective-permute-start | bytes 393224 | tf_op jit(solution)/shard_map/ppermute | solution.py:60
  46.0 7.2 %collective-permute-start.6 = (f32[1,128,256]{2,1,0:T(8,128)S(1)}, f32[1,128,256]{2,1,0:T(8,128)S(1)}, u32[]{:S(2)}, u32[]{:S(2)}) collective-permute-start(f32[1,128,256]{2,1,0:T(8,128)S(1)} %collective-permute-done.4), channel_id=1, source_target_pairs={{0,2},{2,4},{4,6},{6,8},{8,10},{10,12},{12,14},{14,16},{16,18},{18... | collective-permute-start | bytes 393224 | tf_op jit(solution)/shard_map/ppermute | solution.py:53
  46.0 7.2 %collective-permute-start.7 = (f32[1,128,256]{2,1,0:T(8,128)S(1)}, f32[1,128,256]{2,1,0:T(8,128)S(1)}, u32[]{:S(2)}, u32[]{:S(2)}) collective-permute-start(f32[1,128,256]{2,1,0:T(8,128)S(1)} %collective-permute-done.5), channel_id=1, source_target_pairs={{0,30},{2,0},{4,2},{6,4},{8,6},{10,8},{12,10},{14,12},{16,14},{18,... | collective-permute-start | bytes 393224 | tf_op jit(solution)/shard_map/ppermute | solution.py:60
  53.2 7.2 %collective-permute-start.8 = (f32[1,128,256]{2,1,0:T(8,128)S(1)}, f32[1,128,256]{2,1,0:T(8,128)S(1)}, u32[]{:S(2)}, u32[]{:S(2)}) collective-permute-start(f32[1,128,256]{2,1,0:T(8,128)S(1)} %collective-permute-done.6), channel_id=1, source_target_pairs={{0,2},{2,4},{4,6},{6,8},{8,10},{10,12},{12,14},{14,16},{16,18},{18... | collective-permute-start | bytes 393224 | tf_op jit(solution)/shard_map/ppermute | solution.py:53
  53.2 7.2 %collective-permute-start.9 = (f32[1,128,256]{2,1,0:T(8,128)S(1)}, f32[1,128,256]{2,1,0:T(8,128)S(1)}, u32[]{:S(2)}, u32[]{:S(2)}) collective-permute-start(f32[1,128,256]{2,1,0:T(8,128)S(1)} %collective-permute-done.7), channel_id=1, source_target_pairs={{0,30},{2,0},{4,2},{6,4},{8,6},{10,8},{12,10},{14,12},{16,14},{18,... | collective-permute-start | bytes 393224 | tf_op jit(solution)/shard_map/ppermute | solution.py:60
  60.4 7.2 %collective-permute-start.10 = (f32[1,128,256]{2,1,0:T(8,128)S(1)}, f32[1,128,256]{2,1,0:T(8,128)S(1)}, u32[]{:S(2)}, u32[]{:S(2)}) collective-permute-start(f32[1,128,256]{2,1,0:T(8,128)S(1)} %collective-permute-done.8), channel_id=1, source_target_pairs={{0,2},{2,4},{4,6},{6,8},{8,10},{10,12},{12,14},{14,16},{16,18},{18... | collective-permute-start | bytes 393224 | tf_op jit(solution)/shard_map/ppermute | solution.py:53
  60.4 7.2 %collective-permute-start.11 = (f32[1,128,256]{2,1,0:T(8,128)S(1)}, f32[1,128,256]{2,1,0:T(8,128)S(1)}, u32[]{:S(2)}, u32[]{:S(2)}) collective-permute-start(f32[1,128,256]{2,1,0:T(8,128)S(1)} %collective-permute-done.9), channel_id=1, source_target_pairs={{0,30},{2,0},{4,2},{6,4},{8,6},{10,8},{12,10},{14,12},{16,14},{18,... | collective-permute-start | bytes 393224 | tf_op jit(solution)/shard_map/ppermute | solution.py:60
  101.4 93.8 %reduce-scatter.7.cloned.1.call-start = ((), (), s32[]{:S(2)}) async-start(), calls=%async_computation.5 | async-start | bytes 393216 | tf_op jit(solution)/shard_map/reduce_scatter | solution.py:31
  112.0 7.2 %collective-permute-start.15 = (f32[1,128,256]{2,1,0:T(8,128)S(1)}, f32[1,128,256]{2,1,0:T(8,128)S(1)}, u32[]{:S(2)}, u32[]{:S(2)}) collective-permute-start(f32[1,128,256]{2,1,0:T(8,128)S(1)} %bitcast.216), channel_id=1, source_target_pairs={{0,2},{2,4},{4,6},{6,8},{8,10},{10,12},{12,14},{14,16},{16,18},{18... | collective-permute-start | bytes 393224 | tf_op jit(solution)/shard_map/ppermute | solution.py:53
  126.4 7.2 %collective-permute-start.19 = (f32[1,128,256]{2,1,0:T(8,128)S(1)}, f32[1,128,256]{2,1,0:T(8,128)S(1)}, u32[]{:S(2)}, u32[]{:S(2)}) collective-permute-start(f32[1,128,256]{2,1,0:T(8,128)S(1)} %collective-permute-done.17), channel_id=1, source_target_pairs={{0,2},{2,4},{4,6},{6,8},{8,10},{10,12},{12,14},{14,16},{16,18},{18... | collective-permute-start | bytes 393224 | tf_op jit(solution)/shard_map/ppermute | solution.py:53
  133.6 7.2 %collective-permute-start.21 = (f32[1,128,256]{2,1,0:T(8,128)S(1)}, f32[1,128,256]{2,1,0:T(8,128)S(1)}, u32[]{:S(2)}, u32[]{:S(2)}) collective-permute-start(f32[1,128,256]{2,1,0:T(8,128)S(1)} %collective-permute-done.19), channel_id=1, source_target_pairs={{0,2},{2,4},{4,6},{6,8},{8,10},{10,12},{12,14},{14,16},{16,18},{18... | collective-permute-start | bytes 393224 | tf_op jit(solution)/shard_map/ppermute | solution.py:53
  140.8 7.2 %collective-permute-start.23 = (f32[1,128,256]{2,1,0:T(8,128)S(1)}, f32[1,128,256]{2,1,0:T(8,128)S(1)}, u32[]{:S(2)}, u32[]{:S(2)}) collective-permute-start(f32[1,128,256]{2,1,0:T(8,128)S(1)} %collective-permute-done.21), channel_id=1, source_target_pairs={{0,2},{2,4},{4,6},{6,8},{8,10},{10,12},{12,14},{14,16},{16,18},{18... | collective-permute-start | bytes 393224 | tf_op jit(solution)/shard_map/ppermute | solution.py:53
  148.0 7.2 %collective-permute-start.25 = (f32[1,128,256]{2,1,0:T(8,128)S(1)}, f32[1,128,256]{2,1,0:T(8,128)S(1)}, u32[]{:S(2)}, u32[]{:S(2)}) collective-permute-start(f32[1,128,256]{2,1,0:T(8,128)S(1)} %collective-permute-done.23), channel_id=1, source_target_pairs={{0,2},{2,4},{4,6},{6,8},{8,10},{10,12},{12,14},{14,16},{16,18},{18... | collective-permute-start | bytes 393224 | tf_op jit(solution)/shard_map/ppermute | solution.py:53
  187.3 92.0 %reduce-scatter.9.cloned.1.call-start = ((), (), s32[]{:S(2)}) async-start(), calls=%async_computation.6 | async-start | bytes 393216 | tf_op jit(solution)/shard_map/reduce_scatter | solution.py:31
  196.3 7.2 %collective-permute-start.30 = (f32[1,128,256]{2,1,0:T(8,128)S(1)}, f32[1,128,256]{2,1,0:T(8,128)S(1)}, u32[]{:S(2)}, u32[]{:S(2)}) collective-permute-start(f32[1,128,256]{2,1,0:T(8,128)S(1)} %bitcast.208), channel_id=1, source_target_pairs={{0,2},{2,4},{4,6},{6,8},{8,10},{10,12},{12,14},{14,16},{16,18},{18... | collective-permute-start | bytes 393224 | tf_op jit(solution)/shard_map/ppermute | solution.py:53
  196.4 7.2 %collective-permute-start.31 = (f32[1,128,256]{2,1,0:T(8,128)S(1)}, f32[1,128,256]{2,1,0:T(8,128)S(1)}, u32[]{:S(2)}, u32[]{:S(2)}) collective-permute-start(f32[1,128,256]{2,1,0:T(8,128)S(1)} %bitcast.209), channel_id=1, source_target_pairs={{0,30},{2,0},{4,2},{6,4},{8,6},{10,8},{12,10},{14,12},{16,14},{18,... | collective-permute-start | bytes 393224 | tf_op jit(solution)/shard_map/ppermute | solution.py:60
  210.7 7.2 %collective-permute-start.34 = (f32[1,128,256]{2,1,0:T(8,128)S(1)}, f32[1,128,256]{2,1,0:T(8,128)S(1)}, u32[]{:S(2)}, u32[]{:S(2)}) collective-permute-start(f32[1,128,256]{2,1,0:T(8,128)S(1)} %collective-permute-done.32), channel_id=1, source_target_pairs={{0,2},{2,4},{4,6},{6,8},{8,10},{10,12},{12,14},{14,16},{16,18},{18... | collective-permute-start | bytes 393224 | tf_op jit(solution)/shard_map/ppermute | solution.py:53
  217.9 7.2 %collective-permute-start.36 = (f32[1,128,256]{2,1,0:T(8,128)S(1)}, f32[1,128,256]{2,1,0:T(8,128)S(1)}, u32[]{:S(2)}, u32[]{:S(2)}) collective-permute-start(f32[1,128,256]{2,1,0:T(8,128)S(1)} %collective-permute-done.34), channel_id=1, source_target_pairs={{0,2},{2,4},{4,6},{6,8},{8,10},{10,12},{12,14},{14,16},{16,18},{18... | collective-permute-start | bytes 393224 | tf_op jit(solution)/shard_map/ppermute | solution.py:53
  225.1 7.2 %collective-permute-start.38 = (f32[1,128,256]{2,1,0:T(8,128)S(1)}, f32[1,128,256]{2,1,0:T(8,128)S(1)}, u32[]{:S(2)}, u32[]{:S(2)}) collective-permute-start(f32[1,128,256]{2,1,0:T(8,128)S(1)} %collective-permute-done.36), channel_id=1, source_target_pairs={{0,2},{2,4},{4,6},{6,8},{8,10},{10,12},{12,14},{14,16},{16,18},{18... | collective-permute-start | bytes 393224 | tf_op jit(solution)/shard_map/ppermute | solution.py:53
  232.2 7.2 %collective-permute-start.40 = (f32[1,128,256]{2,1,0:T(8,128)S(1)}, f32[1,128,256]{2,1,0:T(8,128)S(1)}, u32[]{:S(2)}, u32[]{:S(2)}) collective-permute-start(f32[1,128,256]{2,1,0:T(8,128)S(1)} %collective-permute-done.38), channel_id=1, source_target_pairs={{0,2},{2,4},{4,6},{6,8},{8,10},{10,12},{12,14},{14,16},{16,18},{18... | collective-permute-start | bytes 393224 | tf_op jit(solution)/shard_map/ppermute | solution.py:53
  271.4 92.2 %reduce-scatter.11.cloned.1.call-start = ((), (), s32[]{:S(2)}) async-start(), calls=%async_computation.7 | async-start | bytes 393216 | tf_op jit(solution)/shard_map/reduce_scatter | solution.py:31
  280.5 7.2 %collective-permute-start.45 = (f32[1,128,256]{2,1,0:T(8,128)S(1)}, f32[1,128,256]{2,1,0:T(8,128)S(1)}, u32[]{:S(2)}, u32[]{:S(2)}) collective-permute-start(f32[1,128,256]{2,1,0:T(8,128)S(1)} %bitcast.211), channel_id=1, source_target_pairs={{0,2},{2,4},{4,6},{6,8},{8,10},{10,12},{12,14},{14,16},{16,18},{18... | collective-permute-start | bytes 393224 | tf_op jit(solution)/shard_map/ppermute | solution.py:53
  294.8 7.2 %collective-permute-start.49 = (f32[1,128,256]{2,1,0:T(8,128)S(1)}, f32[1,128,256]{2,1,0:T(8,128)S(1)}, u32[]{:S(2)}, u32[]{:S(2)}) collective-permute-start(f32[1,128,256]{2,1,0:T(8,128)S(1)} %collective-permute-done.47), channel_id=1, source_target_pairs={{0,2},{2,4},{4,6},{6,8},{8,10},{10,12},{12,14},{14,16},{16,18},{18... | collective-permute-start | bytes 393224 | tf_op jit(solution)/shard_map/ppermute | solution.py:53
  302.0 7.2 %collective-permute-start.51 = (f32[1,128,256]{2,1,0:T(8,128)S(1)}, f32[1,128,256]{2,1,0:T(8,128)S(1)}, u32[]{:S(2)}, u32[]{:S(2)}) collective-permute-start(f32[1,128,256]{2,1,0:T(8,128)S(1)} %collective-permute-done.49), channel_id=1, source_target_pairs={{0,2},{2,4},{4,6},{6,8},{8,10},{10,12},{12,14},{14,16},{16,18},{18... | collective-permute-start | bytes 393224 | tf_op jit(solution)/shard_map/ppermute | solution.py:53
  309.2 7.2 %collective-permute-start.53 = (f32[1,128,256]{2,1,0:T(8,128)S(1)}, f32[1,128,256]{2,1,0:T(8,128)S(1)}, u32[]{:S(2)}, u32[]{:S(2)}) collective-permute-start(f32[1,128,256]{2,1,0:T(8,128)S(1)} %collective-permute-done.51), channel_id=1, source_target_pairs={{0,2},{2,4},{4,6},{6,8},{8,10},{10,12},{12,14},{14,16},{16,18},{18... | collective-permute-start | bytes 393224 | tf_op jit(solution)/shard_map/ppermute | solution.py:53
  316.4 7.2 %collective-permute-start.55 = (f32[1,128,256]{2,1,0:T(8,128)S(1)}, f32[1,128,256]{2,1,0:T(8,128)S(1)}, u32[]{:S(2)}, u32[]{:S(2)}) collective-permute-start(f32[1,128,256]{2,1,0:T(8,128)S(1)} %collective-permute-done.53), channel_id=1, source_target_pairs={{0,2},{2,4},{4,6},{6,8},{8,10},{10,12},{12,14},{14,16},{16,18},{18... | collective-permute-start | bytes 393224 | tf_op jit(solution)/shard_map/ppermute | solution.py:53
  316.4 7.2 %collective-permute-start.56 = (f32[1,128,256]{2,1,0:T(8,128)S(1)}, f32[1,128,256]{2,1,0:T(8,128)S(1)}, u32[]{:S(2)}, u32[]{:S(2)}) collective-permute-start(f32[1,128,256]{2,1,0:T(8,128)S(1)} %collective-permute-done.54), channel_id=1, source_target_pairs={{0,30},{2,0},{4,2},{6,4},{8,6},{10,8},{12,10},{14,12},{16,14},{18,... | collective-permute-start | bytes 393224 | tf_op jit(solution)/shard_map/ppermute | solution.py:60
  323.7 7.2 %collective-permute-start.58 = (f32[1,128,256]{2,1,0:T(8,128)S(1)}, f32[1,128,256]{2,1,0:T(8,128)S(1)}, u32[]{:S(2)}, u32[]{:S(2)}) collective-permute-start(f32[1,128,256]{2,1,0:T(8,128)S(1)} %collective-permute-done.56), channel_id=1, source_target_pairs={{0,30},{2,0},{4,2},{6,4},{8,6},{10,8},{12,10},{14,12},{16,14},{18,... | collective-permute-start | bytes 393224 | tf_op jit(solution)/shard_map/ppermute | solution.py:60
  (39 other events, 271.5 us)
Sparse Core Ops, SparseCore 0:
  101.5 9.3 reduce-scatter.4
  187.4 7.7 reduce-scatter.6
  271.5 7.7 reduce-scatter.8
  355.9 7.7 reduce-scatter.10
